TPU v7x, 512 devices: a whole 4x8x8 slice. The times are simulated.
512 devices in a mesh: fsdp: 32 (over y, z_hi), tp: 16 (over x, z_lo, core).
Axes of the slice: x: 4, y: 8, z: 8 (z_hi: 4, z_lo: 2; z = z_hi * 2 + z_lo), core: 2. Of those that a mesh axis runs over, the one named last changes fastest.
Arguments:
- acts: bfloat16 [8192, 4096], P('fsdp'), may hold values from -6 to 6
- cots: bfloat16 [8192, 14336], P('fsdp', 'tp'), may hold values from -6 to 6
- weight: bfloat16 [4096, 14336], P('fsdp', 'tp'), may hold values from -0.09375 to 0.09375
- basis_in: bfloat16 [32, 128, 128], P('fsdp'), may hold values from -0.5 to 0.5
- basis_out: bfloat16 [16, 896, 896], P('tp', 'fsdp'), may hold values from -0.1875 to 0.1875
- eigen_in: float32 [4096], P('fsdp'), may hold values from 0.2 to 5
- eigen_out: float32 [14336], P('tp'), may hold values from 0.2 to 5
- forget_rows: int32 [2048], P('fsdp'), may hold values from 0 to 255
- retain_rows: int32 [1024], P('fsdp'), may hold values from 0 to 255
Outputs:
- retained: bfloat16 [1024, 14336], P('fsdp', 'tp')
- back_grads: bfloat16 [1024, 4096], P('fsdp')
All inputs are finite; a program needn't handle non-finite values.
Results may differ from a plain program's by a relative error of at most 0.022.
Values may be sent and summed in bfloat16 or wider, within the bound.
A program may use at most 64 MiB of HBM per device.

v0:
```python
import jax
import jax.numpy as jnp
from jax import lax
from jax.sharding import PartitionSpec as P

damping = 0.1
step_size = 0.5


def shards(acts, cots, weight, basis_in, basis_out, eigen_in, eigen_out, forget_rows, retain_rows):
    fsdp_count = lax.axis_size("fsdp")
    forget_local = forget_rows.shape[0]
    forget_count = forget_local * fsdp_count
    row_count = weight.shape[0]
    col_count = weight.shape[1]
    in_blocks = basis_in.shape[0]
    in_order = basis_in.shape[1]
    forget_acts = jnp.take(acts, forget_rows, axis=0)
    forget_cots = jnp.take(cots, forget_rows, axis=0)
    basis_full = lax.all_gather(basis_out, "fsdp", axis=1, tiled=True)
    out_blocks = basis_full.shape[0]
    out_order = basis_full.shape[2]
    rotated_cots = (
        jnp.einsum(
            "tgi,gij->tgj",
            forget_cots.reshape(forget_local, out_blocks, out_order),
            basis_full,
            preferred_element_type=jnp.float32,
        )
        .reshape(forget_local, col_count)
        .astype(jnp.bfloat16)
    )
    feature_cols = lax.all_to_all(forget_acts, "fsdp", split_axis=1, concat_axis=0, tiled=True)
    rotated_acts = (
        jnp.einsum(
            "tbi,bij->tbj",
            feature_cols.reshape(forget_count, in_blocks, in_order),
            basis_in,
            preferred_element_type=jnp.float32,
        )
        .reshape(forget_count, row_count)
        .astype(jnp.bfloat16)
    )
    moments = (
        lax.dot_general(
            rotated_acts,
            lax.all_gather(rotated_cots, "fsdp", axis=0, tiled=True),
            (((0,), (0,)), ((), ())),
            preferred_element_type=jnp.float32,
        )
        / forget_count
    )
    damped = eigen_in[:, None] * eigen_out[None, :] + damping
    scaled = (moments / damped).astype(jnp.bfloat16)
    back_out = (
        jnp.einsum(
            "dgi,gji->dgj",
            scaled.reshape(row_count, out_blocks, out_order),
            basis_full,
            preferred_element_type=jnp.float32,
        )
        .reshape(row_count, col_count)
        .astype(jnp.bfloat16)
    )
    update = jnp.einsum(
        "bij,bjc->bic",
        basis_in,
        back_out.reshape(in_blocks, in_order, col_count),
        preferred_element_type=jnp.float32,
    ).reshape(row_count, col_count)
    new_weight = (weight.astype(jnp.float32) + step_size * update).astype(jnp.bfloat16)
    retain_acts = jnp.take(acts, retain_rows, axis=0)
    retain_cots = jnp.take(cots, retain_rows, axis=0)
    retain_cols = lax.all_to_all(retain_acts, "fsdp", split_axis=1, concat_axis=0, tiled=True)
    retained = lax.psum_scatter(
        jnp.dot(retain_cols, new_weight, preferred_element_type=jnp.float32).astype(jnp.bfloat16),
        "fsdp",
        scatter_dimension=0,
        tiled=True,
    )
    grad_cols = lax.dot_general(
        lax.all_gather(retain_cots, "fsdp", axis=0, tiled=True),
        new_weight,
        (((1,), (1,)), ((), ())),
        preferred_element_type=jnp.float32,
    )
    grad_summed = lax.psum(grad_cols.astype(jnp.bfloat16), "tp")
    back_grads = lax.all_to_all(grad_summed, "fsdp", split_axis=0, concat_axis=1, tiled=True)
    return (retained, back_grads)


def solution(mesh):
    placed = (
        P("fsdp", None),
        P("fsdp", "tp"),
        P("fsdp", "tp"),
        P("fsdp", None, None),
        P("tp", "fsdp", None),
        P("fsdp"),
        P("tp"),
        P("fsdp"),
        P("fsdp"),
    )
    return jax.shard_map(
        shards,
        mesh=mesh,
        in_specs=placed,
        out_specs=(P("fsdp", "tp"), P("fsdp", None)),
        check_vma=False,
    )
```

profile of v0, /device:TPU:2, one launch (start us, length us, event | category | flops | bytes accessed | tf_op | source)
XLA Modules:
  0.0 666.9 jit_solution(1411980744719282719)
XLA Ops:
  7.2 0.0 copy-start
  7.2 0.0 copy-start.1
  7.2 0.0 copy-start.5
  7.2 0.0 all-gather.4.cloned.1.call-start
  7.2 1.7 copy.25
  8.9 0.0 all-gather.4.cloned.1.call-update
  9.0 0.0 all-gather.6.cloned.1.call-start
  9.0 0.7 compare_select_fusion
  9.7 1.9 gather_fusion.2
  11.5 0.7 compare_and_fusion
  12.2 99.0 %all-gather.4.cloned.1.call-done = bf16[1,896,896]{2,0,1:T(2,128)(2,1)} async-done(((bf16[1,28,896]{2,0,1:T(2,128)(2,1)}), bf16[1,896,896]{2,0,1:T(2,128)(2,1)}) %all-gather.4.cloned.1.call-update) | async-done | bytes 1605648 | tf_op jit(solution)/shard_map/all_gather | solution.py:20
  111.2 3.0 fusion.16
  114.2 0.0 all-gather.6.cloned.1.call-update
  114.2 0.0 all-gather.8.cloned.1.call-start
  114.2 0.0 copy-done.5
  114.3 0.0 copy-done.1
  114.3 0.6 gather_fusion.3
  114.9 0.7 broadcast_select_fusion
  115.6 0.0 all-gather.8.cloned.1.call-update
  115.7 0.0 copy-done
  115.7 0.9 gather_fusion.1
  116.5 0.0 copy-start.2
  116.6 1.1 bitcast_select_fusion
  117.6 6.8 %all-to-all-start.1 = ((bf16[64,32,128]{2,0,1:T(8,128)(2,1)}), bf16[64,32,128]{2,0,1:T(8,128)(2,1)S(1)}, u32[]{:S(2)}, u32[]{:S(2)}) async-start(bf16[64,32,128]{2,0,1:T(8,128)(2,1)} %bitcast_select_fusion), calls=%async_computation.1 | async-start | bytes 1048576 | tf_op jit(solution)/shard_map/all_to_all | solution.py:33
  124.4 0.0 copy-start.3
  124.5 0.0 copy-start.4
  124.5 0.0 copy-start.6
  124.5 0.7 gather_fusion
  125.2 0.0 copy-done.2
  125.2 0.2 copy.23
  125.4 0.8 bitcast_select_fusion.1
  126.2 16.7 %all-to-all-done.1 = bf16[64,32,128]{2,0,1:T(8,128)(2,1)S(1)} async-done(((bf16[64,32,128]{2,0,1:T(8,128)(2,1)}), bf16[64,32,128]{2,0,1:T(8,128)(2,1)S(1)}, u32[]{:S(2)}, u32[]{:S(2)}) %all-to-all-start.1) | async-done | bytes 524320 | tf_op jit(solution)/shard_map/all_to_all | solution.py:33
  142.9 5.6 all-to-all-start
  148.6 0.0 all-reduce.2.cloned.1.call-start
  148.6 66.9 %all-gather.6.cloned.1.call-done = bf16[2048,896]{1,0:T(8,128)(2,1)} async-done(((bf16[64,896]{1,0:T(8,128)(2,1)}), bf16[2048,896]{1,0:T(8,128)(2,1)}) %all-gather.6.cloned.1.call-update) | async-done | bytes 3670032 | tf_op jit(solution)/shard_map/all_gather | solution.py:47
  215.6 0.0 copy-done.3
  215.6 0.0 copy-done.4
  215.6 0.0 copy-done.6
  215.6 3.0 fusion.13
  218.6 2.8 fusion.12
  221.4 78.9 %all-gather.8.cloned.1.call-done = bf16[1024,896]{1,0:T(8,128)(2,1)} async-done(((bf16[32,896]{1,0:T(8,128)(2,1)}), bf16[1024,896]{1,0:T(8,128)(2,1)}) %all-gather.8.cloned.1.call-update) | async-done | bytes 1835024 | tf_op jit(solution)/shard_map/all_gather | solution.py:82
  300.3 2.9 convolution_convert_fusion.2
  303.1 0.0 all-reduce.2.cloned.1.call-update
  303.2 0.0 reduce-scatter.2.cloned.1.call-start
  303.2 0.0 all-to-all-done
  303.2 1.9 convolution_convert_fusion.1
  305.1 0.0 reduce-scatter.2.cloned.1.call-update
  305.1 116.9 %all-reduce.2.cloned.1.call-done = bf16[32,32,128]{2,1,0:T(8,128)(2,1)} async-done(((bf16[32,32,128]{2,1,0:T(8,128)(2,1)}), bf16[32,32,128]{2,1,0:T(8,128)(2,1)}) %all-reduce.2.cloned.1.call-update) | async-done | bytes 262160 | tf_op jit(solution)/shard_map/psum | solution.py:87
  422.1 25.1 %all_to_all.48 = bf16[32,32,128]{2,1,0:T(8,128)(2,1)S(1)} all-to-all(bf16[32,32,128]{2,1,0:T(8,128)(2,1)} %all-reduce.2.cloned.1.call-done), channel_id=1, replica_groups=mesh['fsdp'=32,'tp'=16] {'fsdp'}, dimensions={0} | all-to-all | bytes 524288 | tf_op jit(solution)/shard_map/all_to_all | solution.py:88
  447.1 0.7 copy_bitcast_fusion
  447.8 212.5 %reduce-scatter.2.cloned.1.call-done = bf16[32,896]{1,0:T(8,128)(2,1)} async-done(((bf16[1024,896]{1,0:T(8,128)(2,1)}), bf16[32,896]{1,0:T(8,128)(2,1)}) %reduce-scatter.2.cloned.1.call-update) | async-done | bytes 57360 | tf_op jit(solution)/shard_map/reduce_scatter | solution.py:75
  (4 shorter events, 0.0 us)
Async XLA Ops:
  7.2 108.5 %copy-start = (bf16[256,4096]{1,0:T(8,128)(2,1)S(1)}, bf16[256,4096]{1,0:T(8,128)(2,1)}, u32[]{:S(2)}) copy-start(bf16[256,4096]{1,0:T(8,128)(2,1)} %param.9) | copy-start | bytes 6291460
  7.2 107.1 %copy-start.1 = (bf16[256,896]{1,0:T(8,128)(2,1)S(1)}, bf16[256,896]{1,0:T(8,128)(2,1)}, u32[]{:S(2)}) copy-start(bf16[256,896]{1,0:T(8,128)(2,1)} %param.10) | copy-start | bytes 1376260
  7.2 107.0 %copy-start.5 = (s32[32]{0:T(128)S(1)}, s32[32]{0:T(128)}, u32[]{:S(2)}) copy-start(s32[32]{0:T(128)} %param.17) | copy-start | bytes 388
  7.2 104.0 %all-gather.4.cloned.1.call-start = ((), (), s32[]{:S(2)}) async-start(), calls=%async_computation.4 | async-start | bytes 3311616 | tf_op jit(solution)/shard_map/all_gather | solution.py:20
  9.0 206.6 %all-gather.6.cloned.1.call-start = ((), (), s32[]{:S(2)}) async-start(), calls=%async_computation.5 | async-start | bytes 3784704 | tf_op jit(solution)/shard_map/all_gather | solution.py:47
  114.2 186.1 %all-gather.8.cloned.1.call-start = ((), (), s32[]{:S(2)}) async-start(), calls=%async_computation.7 | async-start | bytes 1892352 | tf_op jit(solution)/shard_map/all_gather | solution.py:82
  116.5 8.7 %copy-start.2 = (bf16[128,896]{1,0:T(8,128)(2,1)S(1)}, bf16[128,896]{1,0:T(8,128)(2,1)}, u32[]{:S(2)}) copy-start(bf16[128,896]{1,0:T(8,128)(2,1)} %param.11) | copy-start | bytes 688132
  117.6 25.3 %all-to-all-start.1 = ((bf16[64,32,128]{2,0,1:T(8,128)(2,1)}), bf16[64,32,128]{2,0,1:T(8,128)(2,1)S(1)}, u32[]{:S(2)}, u32[]{:S(2)}) async-start(bf16[64,32,128]{2,0,1:T(8,128)(2,1)} %bitcast_select_fusion), calls=%async_computation.1 | async-start | bytes 1048576 | tf_op jit(solution)/shard_map/all_to_all | solution.py:33
  124.4 91.1 %copy-start.3 = (bf16[1,128,128]{2,1,0:T(8,128)(2,1)S(1)}, bf16[1,128,128]{2,1,0:T(8,128)(2,1)}, u32[]{:S(2)}) copy-start(bf16[1,128,128]{2,1,0:T(8,128)(2,1)} %param.12) | copy-start | bytes 98308
  124.5 91.1 %copy-start.4 = (f32[896]{0:T(1024)S(1)}, f32[896]{0:T(1024)}, u32[]{:S(2)}) copy-start(f32[896]{0:T(1024)} %param.15) | copy-start | bytes 10756
  124.5 91.1 %copy-start.6 = (f32[128]{0:T(128)S(1)}, f32[128]{0:T(128)}, u32[]{:S(2)}) copy-start(f32[128]{0:T(128)} %param.14) | copy-start | bytes 1540
  142.9 160.3 %all-to-all-start = ((bf16[32,32,128]{2,0,1:T(8,128)(2,1)}), bf16[32,32,128]{2,0,1:T(8,128)(2,1)S(1)}, u32[]{:S(2)}, u32[]{:S(2)}) async-start(bf16[32,32,128]{2,0,1:T(8,128)(2,1)} %bitcast_select_fusion.1), calls=%async_computation | async-start | bytes 524288 | tf_op jit(solution)/shard_map/all_to_all | solution.py:74
  148.6 273.5 %all-reduce.2.cloned.1.call-start = ((), (), s32[]{:S(2)}) async-start(), calls=%async_computation.8 | async-start | bytes 524288 | tf_op jit(solution)/shard_map/psum | solution.py:87
  303.2 357.2 %reduce-scatter.2.cloned.1.call-start = ((), (), s32[]{:S(2)}) async-start(), calls=%async_computation.6 | async-start | bytes 1892352 | tf_op jit(solution)/shard_map/reduce_scatter | solution.py:75
Sparse Core Ops, SparseCore 0:
  11.7 99.4 all-gather.3
  114.4 101.1 all-gather.5
  219.3 80.9 all-gather.7
  303.3 118.7 all-reduce.1
  427.6 232.6 reduce-scatter.1
where the time goes:
time: 667 us
  waiting for transfers between devices  591 us (89%)
  blocking collectives  25.1 us (4%)
  between operations  14 us (2%)
  matrix products  13.6 us (2%)
  starting transfers between devices  12.7 us (2%)
  local copies, waits for them, and re-layouts  6.69 us (1%)
    reduce_scatter x1, waiting for transfers between devices, shards(): lax.psum_scatter(jnp.dot(retain_cols, new_weight, preferred_element_type=...  213 us
    psum x1, waiting for transfers between devices, shards(): grad_summed = lax.psum(grad_cols.astype(jnp.bfloat16), 'tp')  117 us
    all_gather x1, waiting for transfers between devices, shards(): basis_full = lax.all_gather(basis_out, 'fsdp', axis=1, tiled=True)  99 us
    all_gather x1, waiting for transfers between devices, shards(): lax.all_gather(retain_cots, 'fsdp', axis=0, tiled=True)  78.9 us
    all_gather x1, waiting for transfers between devices, shards(): lax.all_gather(rotated_cots, 'fsdp', axis=0, tiled=True)  66.9 us
    all_to_all x1, blocking collectives, shards(): lax.all_to_all(grad_summed, 'fsdp', split_axis=0, concat_axis=1, tiled=True)  25.1 us
    all_to_all x1, waiting for transfers between devices, shards(): lax.all_to_all(forget_acts, 'fsdp', split_axis=1, concat_axis=0, tiled=True)  16.7 us
  transfers between devices with their start and end apart: 7, of which 6 were waited for; matrix products, arithmetic and copies ran while one was open for 3% of the time, Pallas kernels for 0%

commit v1 on v0

--- a/solution.py
+++ b/solution.py
@@ -84,7 +84,8 @@
         (((1,), (1,)), ((), ())),
         preferred_element_type=jnp.float32,
     )
-    grad_summed = lax.psum(grad_cols.astype(jnp.bfloat16), "tp")
+    field = grad_cols.astype(jnp.bfloat16)
+    grad_summed = jnp.sum(lax.all_gather(field, "tp"), axis=0)
     back_grads = lax.all_to_all(grad_summed, "fsdp", split_axis=0, concat_axis=1, tiled=True)
     return (retained, back_grads)
 

time: 667 us -> 583 us (0.87)
  waiting for transfers between devices: 591 us -> 491 us
  blocking collectives: 25.1 us -> 44.2 us
    psum x1 -> x0, waiting for transfers between devices: 117 us -> none  [shards(): grad_summed = lax.psum(grad_cols.astype(jnp.bfloat16), 'tp')]
    all_to_all x0 -> x1, blocking collectives: none -> 20.2 us  [shards(): lax.all_to_all(retain_acts, 'fsdp', split_axis=1, concat_axis=0, tiled=True)]
    all_gather x0 -> x1, waiting for transfers between devices: none -> 18.8 us  [shards(): grad_summed = jnp.sum(lax.all_gather(field, 'tp'), axis=0)]
    reduce_scatter x1, waiting for transfers between devices: 213 us -> 204 us  [shards(): lax.psum_scatter(jnp.dot(retain_cols, new_weight, preferred_element_type=...]
  transfers between devices with their start and end apart: 7 -> 6, of which waited for: 6 -> 6; matrix products, arithmetic and copies ran while one was open for 3% -> 3% of each run, Pallas kernels for 0% -> 0%
where the time goes in v1:
time: 583 us; the launch traced here: 582 us
  waiting for transfers between devices  491 us (84%)
  blocking collectives  44.2 us (8%)
  between operations  13.9 us (2%)
  matrix products  13.6 us (2%)
  starting transfers between devices  7.03 us (1%)
  local copies, waits for them, and re-layouts  6.69 us (1%)
  other arithmetic  6.08 us (1%)
    reduce_scatter x1, waiting for transfers between devices, shards(): lax.psum_scatter(jnp.dot(retain_cols, new_weight, preferred_element_type=...  204 us
    all_gather x1, waiting for transfers between devices, shards(): basis_full = lax.all_gather(basis_out, 'fsdp', axis=1, tiled=True)  99 us
    all_gather x1, waiting for transfers between devices, shards(): lax.all_gather(retain_cots, 'fsdp', axis=0, tiled=True)  78.9 us
    all_gather x1, waiting for transfers between devices, shards(): lax.all_gather(rotated_cots, 'fsdp', axis=0, tiled=True)  71.6 us
    all_to_all x1, blocking collectives, shards(): lax.all_to_all(grad_summed, 'fsdp', split_axis=0, concat_axis=1, tiled=True)  24 us
    all_to_all x1, blocking collectives, shards(): lax.all_to_all(retain_acts, 'fsdp', split_axis=1, concat_axis=0, tiled=True)  20.2 us
    all_gather x1, waiting for transfers between devices, shards(): grad_summed = jnp.sum(lax.all_gather(field, 'tp'), axis=0)  18.8 us
    all_to_all x1, waiting for transfers between devices, shards(): lax.all_to_all(forget_acts, 'fsdp', split_axis=1, concat_axis=0, tiled=True)  18.3 us
  transfers between devices with their start and end apart: 6, of which 6 were waited for; matrix products, arithmetic and copies ran while one was open for 3% of the time, Pallas kernels for 0%

profile of v1, /device:TPU:2, one launch (start us, length us, event | category | flops | bytes accessed | tf_op | source)
XLA Modules:
  0.0 582.0 jit_solution(3757615406161461350)
XLA Ops:
  7.2 0.0 copy-start
  7.2 0.0 copy-start.1
  7.2 0.0 copy-start.5
  7.2 0.0 all-gather.6.cloned.1.call-start
  7.2 1.7 copy.27
  8.9 0.0 all-gather.6.cloned.1.call-update
  9.0 0.0 all-gather.8.cloned.1.call-start
  9.0 0.7 compare_select_fusion
  9.7 1.9 gather_fusion.2
  11.5 0.7 compare_and_fusion
  12.2 99.0 %all-gather.6.cloned.1.call-done = bf16[1,896,896]{2,0,1:T(2,128)(2,1)} async-done(((bf16[1,28,896]{2,0,1:T(2,128)(2,1)}), bf16[1,896,896]{2,0,1:T(2,128)(2,1)}) %all-gather.6.cloned.1.call-update) | async-done | bytes 1605648 | tf_op jit(solution)/shard_map/all_gather | solution.py:20
  111.2 3.0 fusion.16
  114.2 0.0 all-gather.8.cloned.1.call-update
  114.2 0.0 all-gather.10.cloned.1.call-start
  114.2 0.0 copy-done.5
  114.3 0.0 copy-done.1
  114.3 0.6 gather_fusion.3
  114.9 0.7 broadcast_select_fusion
  115.6 0.0 all-gather.10.cloned.1.call-update
  115.7 0.0 copy-done
  115.7 0.9 gather_fusion.1
  116.5 0.0 copy-start.2
  116.6 0.0 copy-start.3
  116.6 0.0 copy-start.4
  116.6 0.0 copy-start.6
  116.6 1.0 bitcast_select_fusion
  117.6 6.8 %all-to-all-start.1 = ((bf16[64,32,128]{2,0,1:T(8,128)(2,1)}), bf16[64,32,128]{2,0,1:T(8,128)(2,1)S(1)}, u32[]{:S(2)}, u32[]{:S(2)}) async-start(bf16[64,32,128]{2,0,1:T(8,128)(2,1)} %bitcast_select_fusion), calls=%async_computation.1 | async-start | bytes 1048576 | tf_op jit(solution)/shard_map/all_to_all | solution.py:33
  124.5 0.0 all-gather.12.cloned.1.call-start
  124.5 0.0 copy-done.2
  124.5 0.2 copy.25
  124.7 18.3 %all-to-all-done.1 = bf16[64,32,128]{2,0,1:T(8,128)(2,1)S(1)} async-done(((bf16[64,32,128]{2,0,1:T(8,128)(2,1)}), bf16[64,32,128]{2,0,1:T(8,128)(2,1)S(1)}, u32[]{:S(2)}, u32[]{:S(2)}) %all-to-all-start.1) | async-done | bytes 524320 | tf_op jit(solution)/shard_map/all_to_all | solution.py:33
  143.0 71.6 %all-gather.8.cloned.1.call-done = bf16[2048,896]{1,0:T(8,128)(2,1)} async-done(((bf16[64,896]{1,0:T(8,128)(2,1)}), bf16[2048,896]{1,0:T(8,128)(2,1)}) %all-gather.8.cloned.1.call-update) | async-done | bytes 3670032 | tf_op jit(solution)/shard_map/all_gather | solution.py:47
  214.5 0.0 copy-done.3
  214.5 0.0 copy-done.4
  214.5 0.0 copy-done.6
  214.5 3.0 fusion.13
  217.6 2.8 fusion.12
  220.4 78.9 %all-gather.10.cloned.1.call-done = bf16[1024,896]{1,0:T(8,128)(2,1)} async-done(((bf16[32,896]{1,0:T(8,128)(2,1)}), bf16[1024,896]{1,0:T(8,128)(2,1)}) %all-gather.10.cloned.1.call-update) | async-done | bytes 1835024 | tf_op jit(solution)/shard_map/all_gather | solution.py:82
  299.3 2.8 convolution_convert_fusion.2
  302.1 0.0 all-gather.12.cloned.1.call-update
  302.1 0.0 reduce-scatter.2.cloned.1.call-start
  302.2 0.7 gather_fusion
  302.9 0.1 bitcast_select_fusion.1
  303.0 20.2 %all_to_all.48 = bf16[32,32,128]{2,0,1:T(8,128)(2,1)S(1)} all-to-all(bf16[32,32,128]{2,0,1:T(8,128)(2,1)S(1)} %bitcast_select_fusion.1), channel_id=1, replica_groups=mesh['fsdp'=32,'tp'=16] {'fsdp'}, dimensions={1} | all-to-all | bytes 524288 | tf_op jit(solution)/shard_map/all_to_all | solution.py:74
  323.2 1.9 convolution_convert_fusion.1
  325.1 0.0 reduce-scatter.2.cloned.1.call-update
  325.1 18.8 %all-gather.12.cloned.1.call-done = bf16[16384,128]{1,0:T(8,128)(2,1)} async-done(((bf16[1024,128]{1,0:T(8,128)(2,1)}), bf16[16384,128]{1,0:T(8,128)(2,1)}) %all-gather.12.cloned.1.call-update) | async-done | bytes 4194320 | tf_op jit(solution)/shard_map/all_gather | solution.py:88
  343.9 2.9 reduce_sum.12
  346.8 24.0 %all_to_all.49 = bf16[32,32,128]{2,1,0:T(8,128)(2,1)S(1)} all-to-all(bf16[32,32,128]{2,1,0:T(8,128)(2,1)S(1)} %bitcast.64), channel_id=1, replica_groups=mesh['fsdp'=32,'tp'=16] {'fsdp'}, dimensions={0} | all-to-all | bytes 524288 | tf_op jit(solution)/shard_map/all_to_all | solution.py:89
  370.8 0.7 copy_bitcast_fusion
  371.5 204.0 %reduce-scatter.2.cloned.1.call-done = bf16[32,896]{1,0:T(8,128)(2,1)} async-done(((bf16[1024,896]{1,0:T(8,128)(2,1)}), bf16[32,896]{1,0:T(8,128)(2,1)}) %reduce-scatter.2.cloned.1.call-update) | async-done | bytes 57360 | tf_op jit(solution)/shard_map/reduce_scatter | solution.py:75
  (4 shorter events, 0.0 us)
Async XLA Ops:
  7.2 108.5 %copy-start = (bf16[256,4096]{1,0:T(8,128)(2,1)S(1)}, bf16[256,4096]{1,0:T(8,128)(2,1)}, u32[]{:S(2)}) copy-start(bf16[256,4096]{1,0:T(8,128)(2,1)} %param.9) | copy-start | bytes 6291460
  7.2 107.1 %copy-start.1 = (bf16[256,896]{1,0:T(8,128)(2,1)S(1)}, bf16[256,896]{1,0:T(8,128)(2,1)}, u32[]{:S(2)}) copy-start(bf16[256,896]{1,0:T(8,128)(2,1)} %param.10) | copy-start | bytes 1376260
  7.2 107.0 %copy-start.5 = (s32[32]{0:T(128)S(1)}, s32[32]{0:T(128)}, u32[]{:S(2)}) copy-start(s32[32]{0:T(128)} %param.17) | copy-start | bytes 388
  7.2 104.0 %all-gather.6.cloned.1.call-start = ((), (), s32[]{:S(2)}) async-start(), calls=%async_computation.4 | async-start | bytes 3311616 | tf_op jit(solution)/shard_map/all_gather | solution.py:20
  9.0 205.6 %all-gather.8.cloned.1.call-start = ((), (), s32[]{:S(2)}) async-start(), calls=%async_computation.5 | async-start | bytes 3784704 | tf_op jit(solution)/shard_map/all_gather | solution.py:47
  114.2 185.1 %all-gather.10.cloned.1.call-start = ((), (), s32[]{:S(2)}) async-start(), calls=%async_computation.7 | async-start | bytes 1892352 | tf_op jit(solution)/shard_map/all_gather | solution.py:82
  116.5 8.0 %copy-start.2 = (bf16[128,896]{1,0:T(8,128)(2,1)S(1)}, bf16[128,896]{1,0:T(8,128)(2,1)}, u32[]{:S(2)}) copy-start(bf16[128,896]{1,0:T(8,128)(2,1)} %param.11) | copy-start | bytes 688132
  116.6 98.0 %copy-start.3 = (bf16[1,128,128]{2,1,0:T(8,128)(2,1)S(1)}, bf16[1,128,128]{2,1,0:T(8,128)(2,1)}, u32[]{:S(2)}) copy-start(bf16[1,128,128]{2,1,0:T(8,128)(2,1)} %param.12) | copy-start | bytes 98308
  116.6 98.0 %copy-start.4 = (f32[896]{0:T(1024)S(1)}, f32[896]{0:T(1024)}, u32[]{:S(2)}) copy-start(f32[896]{0:T(1024)} %param.15) | copy-start | bytes 10756
  116.6 98.0 %copy-start.6 = (f32[128]{0:T(128)S(1)}, f32[128]{0:T(128)}, u32[]{:S(2)}) copy-start(f32[128]{0:T(128)} %param.14) | copy-start | bytes 1540
  117.6 25.3 %all-to-all-start.1 = ((bf16[64,32,128]{2,0,1:T(8,128)(2,1)}), bf16[64,32,128]{2,0,1:T(8,128)(2,1)S(1)}, u32[]{:S(2)}, u32[]{:S(2)}) async-start(bf16[64,32,128]{2,0,1:T(8,128)(2,1)} %bitcast_select_fusion), calls=%async_computation.1 | async-start | bytes 1048576 | tf_op jit(solution)/shard_map/all_to_all | solution.py:33
  124.5 219.4 %all-gather.12.cloned.1.call-start = ((), (), s32[]{:S(2)}) async-start(), calls=%async_computation.8 | async-start | bytes 4456448 | tf_op jit(solution)/shard_map/all_gather | solution.py:88
  302.1 273.4 %reduce-scatter.2.cloned.1.call-start = ((), (), s32[]{:S(2)}) async-start(), calls=%async_computation.6 | async-start | bytes 1892352 | tf_op jit(solution)/shard_map/reduce_scatter | solution.py:75
Sparse Core Ops, SparseCore 0:
  11.7 99.4 all-gather.5
  114.9 99.5 all-gather.7
  218.3 80.9 all-gather.9
  302.3 41.5 all-gather.11
  348.8 226.6 reduce-scatter.1
